TPU v7x, 32 devices: a whole 2x2x4 slice. The times are simulated.
32 devices in a mesh: epoch: 8 (over y, x, core), tile: 4 (over z).
Axes of the slice: x: 2, y: 2, z: 4, core: 2. Of those that a mesh axis runs over, the one named last changes fastest.
Arguments:
- images: bfloat16 [1024, 8192], P('epoch', 'tile')
- coverage: int32 [1024, 64], P('epoch', 'tile'), may hold values from 0 to 128, as said below
Outputs:
- scale_ratio: float32 [1024, 1024], P('epoch', 'tile')
- sky_offset: float32 [1024, 1024], P('epoch', 'tile')
Inputs may be any that keep to these rules, and one draw needn't show every extreme that they name: Covered pixels of a segment are its first ones; the mean coverage differs between groups of segments.
All inputs are finite; a program needn't handle non-finite values.
Results may differ from a plain program's by a relative error of at most 0.0003.
Values may be sent and summed in bfloat16 or wider, within the bound.
A program may use at most 64 MiB of HBM per device.

v0:
```python
import jax
import jax.numpy as jnp
from jax import lax
from jax.sharding import PartitionSpec as P

SEG = 128


def expand_flags(coverage):
    within = lax.broadcasted_iota(jnp.int32, (1, 1, SEG), 2)
    flags = within < coverage[:, :, None]
    return flags.reshape(coverage.shape[0], -1).astype(jnp.bfloat16)


def prepare(images, coverage):
    flags = expand_flags(coverage)
    masked = images * flags
    widened = masked.astype(jnp.float32)
    squared = (widened * widened).astype(jnp.bfloat16)
    return (masked, flags, squared)


def contract(left, right):
    return lax.dot_general(
        left, right, (((1,), (1,)), ((), ())), preferred_element_type=jnp.float32
    )


def pair_sums(local, remote):
    masked_a, flags_a, squared_a = local
    masked_b, flags_b, squared_b = remote
    return jnp.stack(
        [
            contract(flags_a, flags_b),
            contract(masked_a, flags_b),
            contract(flags_a, masked_b),
            contract(masked_a, masked_b),
            contract(flags_a, squared_b),
        ]
    )


def body(images, coverage):
    local = prepare(images, coverage)
    remote = prepare(
        lax.all_gather(images, "epoch", axis=0, tiled=True),
        lax.all_gather(coverage, "epoch", axis=0, tiled=True),
    )
    partial_sums = pair_sums(local, remote)
    totals = lax.psum_scatter(partial_sums, "tile", scatter_dimension=2, tiled=True)
    intersection, flux_i, flux_j, cross, power_j = (
        totals[0],
        totals[1],
        totals[2],
        totals[3],
        totals[4],
    )
    spread = intersection * power_j - flux_j * flux_j
    covariance = intersection * cross - flux_i * flux_j
    scale_ratio = covariance / (spread + intersection + 1.0)
    sky_offset = (flux_i - scale_ratio * flux_j) / (intersection + 1.0)
    return (scale_ratio, sky_offset)


def solution(mesh):
    in_specs = (P("epoch", "tile"), P("epoch", "tile"))
    out_specs = (P("epoch", "tile"), P("epoch", "tile"))
    return jax.shard_map(body, mesh=mesh, in_specs=in_specs, out_specs=out_specs, check_vma=False)
```

profile of v0, /device:TPU:0, one launch (start us, length us, event | category | flops | bytes accessed | tf_op | source)
XLA Modules:
  0.0 120.1 jit_solution(12993511891772602217)
XLA Ops:
  7.2 0.0 all-gather.2.cloned.1.call-start
  7.2 0.7 all-gather.2.cloned.1.call-update
  7.9 0.0 reduce-scatter.2.cloned.1.call-start
  7.9 0.8 copy.7
  8.7 10.7 %all_gather.6 = s32[1024,16]{0,1:T(8,128)S(1)} all-gather(s32[128,16]{0,1:T(8,128)} %param.3), channel_id=1, replica_groups=mesh['epoch'=8,'tile'=4] {'epoch'}, dimensions={0}, use_global_device_ids=true | all-gather | bytes 73728 | tf_op jit(solution)/shard_map/all_gather | solution.py:47
  19.4 0.2 copy.8
  19.6 3.4 %fusion.6 = f32[5,128,1024]{2,1,0:T(8,128)S(1)} fusion(s32[1024,16]{0,1:T(8,128)S(1)} %all_gather.6, s32[128,16]{0,1:T(8,128)} %param.3), kind=kOutput, calls=%fused_computation.10 | convolution fusion | flops 539230208 | bytes 598016 | tf_op jit(solution)/shard_map/dot_general | solution.py:24
  23.1 0.3 lt.49.clone
  23.4 0.5 bitcast_compare_fusion.1
  23.9 2.6 %lt.52.clone = s32[1024,16,128]{2,1,0:T(8,128)S(1)} broadcast(s32[1024,16]{1,0:T(8,128)S(1)} %copy.8), dimensions={0,1} | broadcast | bytes 8454144 | tf_op jit(solution)/shard_map/lt | solution.py:11
  26.5 0.0 copy-start.3
  26.5 4.4 %bitcast_compare_fusion = pred[1024,2048]{1,0:T(32,128)(4,1)S(1)} fusion(s32[128,8,16,128]{3,2,1,0:T(8,128)S(1)} %bitcast.75, s32[2048]{0:T(1024)S(1)} %iota_bitcast_fusion), kind=kLoop, calls=%fused_computation | loop fusion | flops 2097152 | bytes 10493952 | tf_op jit(solution)/shard_map/lt | solution.py:11
  30.9 0.0 copy-start.1
  30.9 1.3 %copy-done.1 = pred[1024,2048]{1,0:T(32,128)(4,1)} copy-done((pred[1024,2048]{1,0:T(32,128)(4,1)}, pred[1024,2048]{1,0:T(32,128)(4,1)S(1)}, u32[]{:S(2)}) %copy-start.1) | copy-done | bytes 2097176
  32.2 0.0 copy-done.3
  32.2 1.6 %fusion.8 = f32[5,128,1024]{2,1,0:T(8,128)S(1)} fusion(f32[5,128,1024]{2,1,0:T(8,128)S(1)} %fusion.6, pred[1024,2048]{1,0:T(32,128)(4,1)S(1)} %bitcast_compare_fusion, pred[128,2048]{1,0:T(32,128)(4,1)S(1)} %bitcast_compare_fusion.1, bf16[128,2048]{1,0:T(8,128)(2,1)S(1)} %copy-done.3), kind=kOutput, calls=%fused_computation.14 | convolution fusion | flops 537133056 | bytes 3407872 | tf_op jit(solution)/shard_map/dot_general | solution.py:24
  33.8 15.5 %all-gather.2.cloned.1.call-done = bf16[1024,2048]{1,0:T(8,128)(2,1)} async-done(((bf16[128,2048]{1,0:T(8,128)(2,1)}), bf16[1024,2048]{1,0:T(8,128)(2,1)}) %all-gather.2.cloned.1.call-update) | async-done | bytes 4194320 | tf_op jit(solution)/shard_map/all_gather | solution.py:46
  49.3 0.0 copy-start.2
  49.3 0.0 copy-start.4
  49.3 4.5 %fusion.7 = f32[5,128,1024]{2,1,0:T(8,128)S(1)} fusion(f32[5,128,1024]{2,1,0:T(8,128)S(1)} %fusion.8, pred[128,2048]{1,0:T(32,128)(4,1)S(1)} %bitcast_compare_fusion.1, pred[1024,2048]{1,0:T(32,128)(4,1)} %copy-done.1, bf16[1024,2048]{1,0:T(8,128)(2,1)} %all-gather.2.cloned.1.call-done), kind=kOutput, calls=%fused_computation.12 | convolution fusion | flops 538968064 | bytes 7077888 | tf_op jit(solution)/shard_map/dot_general | solution.py:24
  53.9 0.0 copy-done.2
  53.9 0.1 copy-done.4
  54.0 1.6 %fusion.9 = f32[5,128,1024]{2,1,0:T(8,128)S(1)} fusion(f32[5,128,1024]{2,1,0:T(8,128)S(1)} %fusion.7, pred[1024,2048]{1,0:T(32,128)(4,1)S(1)} %copy-done.2, bf16[1024,2048]{1,0:T(8,128)(2,1)S(1)} %copy-done.4, pred[128,2048]{1,0:T(32,128)(4,1)S(1)} %bitcast_compare_fusion.1, bf16[128,2048]{1,0:T(8,128)(2,1)S(1)} %copy-done.3), kind=kOutput, calls=%fused_computation.16 | convolution fusion | flops 539230208 | bytes 7602176 | tf_op jit(solution)/shard_map/dot_general | solution.py:24
  55.6 1.9 %fusion.4 = f32[5,128,1024]{2,1,0:T(8,128)S(1)} fusion(f32[5,128,1024]{2,1,0:T(8,128)S(1)} %fusion.9, pred[128,2048]{1,0:T(32,128)(4,1)S(1)} %bitcast_compare_fusion.1, pred[1024,2048]{1,0:T(32,128)(4,1)S(1)} %copy-done.2, bf16[1024,2048]{1,0:T(8,128)(2,1)S(1)} %copy-done.4), kind=kOutput, calls=%fused_computation.8 | convolution fusion | flops 545259520 | bytes 7077888 | tf_op jit(solution)/shard_map/dot_general | solution.py:24
  57.6 0.0 copy-start
  57.6 1.5 %copy-done = f32[5,128,1024]{2,1,0:T(8,128)} copy-done((f32[5,128,1024]{2,1,0:T(8,128)}, f32[5,128,1024]{2,1,0:T(8,128)S(1)}, u32[]{:S(2)}) %copy-start) | copy-done | bytes 2621464
  59.1 0.0 reduce-scatter.2.cloned.1.call-update
  59.1 52.3 %reduce-scatter.2.cloned.1.call-done = f32[5,128,256]{2,1,0:T(8,128)} async-done(((f32[5,128,1024]{2,1,0:T(8,128)}), f32[5,128,256]{2,1,0:T(8,128)}) %reduce-scatter.2.cloned.1.call-update) | async-done | bytes 655376 | tf_op jit(solution)/shard_map/reduce_scatter | solution.py:50
  111.4 1.9 %add_divide_fusion = (f32[128,256]{1,0:T(8,128)}, f32[128,256]{1,0:T(8,128)}) fusion(f32[5,128,256]{2,1,0:T(8,128)} %reduce-scatter.2.cloned.1.call-done), kind=kLoop, calls=%fused_computation.36 | loop fusion | flops 425984 | bytes 917504 | tf_op jit(solution)/shard_map/div | solution.py:61
  (1 shorter events, 0.0 us)
Async XLA Ops:
  7.2 42.2 %all-gather.2.cloned.1.call-start = ((), (), s32[]{:S(2)}) async-start(), calls=%async_computation.1 | async-start | bytes 4718592 | tf_op jit(solution)/shard_map/all_gather | solution.py:46
  7.9 103.5 %reduce-scatter.2.cloned.1.call-start = ((), (), s32[]{:S(2)}) async-start(), calls=%async_computation.2 | async-start | bytes 3276800 | tf_op jit(solution)/shard_map/reduce_scatter | solution.py:50
  26.5 5.7 %copy-start.3 = (bf16[128,2048]{1,0:T(8,128)(2,1)S(1)}, bf16[128,2048]{1,0:T(8,128)(2,1)}, u32[]{:S(2)}) copy-start(bf16[128,2048]{1,0:T(8,128)(2,1)} %param.2) | copy-start | bytes 1572868
  30.9 1.3 %copy-start.1 = (pred[1024,2048]{1,0:T(32,128)(4,1)}, pred[1024,2048]{1,0:T(32,128)(4,1)S(1)}, u32[]{:S(2)}) copy-start(pred[1024,2048]{1,0:T(32,128)(4,1)S(1)} %bitcast_compare_fusion) | copy-start | bytes 6291460
  49.3 4.5 %copy-start.2 = (pred[1024,2048]{1,0:T(32,128)(4,1)S(1)}, pred[1024,2048]{1,0:T(32,128)(4,1)}, u32[]{:S(2)}) copy-start(pred[1024,2048]{1,0:T(32,128)(4,1)} %copy-done.1) | copy-start | bytes 6291460
  49.3 4.7 %copy-start.4 = (bf16[1024,2048]{1,0:T(8,128)(2,1)S(1)}, bf16[1024,2048]{1,0:T(8,128)(2,1)}, u32[]{:S(2)}) copy-start(bf16[1024,2048]{1,0:T(8,128)(2,1)} %all-gather.2.cloned.1.call-done) | copy-start | bytes 12582916
  57.6 1.5 %copy-start = (f32[5,128,1024]{2,1,0:T(8,128)}, f32[5,128,1024]{2,1,0:T(8,128)S(1)}, u32[]{:S(2)}) copy-start(f32[5,128,1024]{2,1,0:T(8,128)S(1)} %fusion.4) | copy-start | bytes 7864324
Sparse Core Ops, SparseCore 0:
  9.9 39.4 all-gather.1
  59.2 52.0 reduce-scatter.1
where the time goes:
time: 120 us
  waiting for transfers between devices  68.5 us (57%)
  between operations  14.1 us (12%)
  matrix products  13.1 us (11%)
  blocking collectives  10.7 us (9%)
  local copies, waits for them, and re-layouts  6.88 us (6%)
  other arithmetic  6.79 us (6%)
    reduce_scatter x1, waiting for transfers between devices, body(): lax.psum_scatter(partial_sums, 'tile', scatter_dimension=2, tiled=True)  52.3 us
    all_gather x1, waiting for transfers between devices, body(): lax.all_gather(images, 'epoch', axis=0, tiled=True)  15.5 us
    dot_general x5, matrix products, contract(): lax.dot_general(left, right, (((1,), (1,)), ((), ())), preferred_element_...  13.1 us
    all_gather x1, blocking collectives, body(): lax.all_gather(coverage, 'epoch', axis=0, tiled=True)  10.7 us
    lt x2, other arithmetic, expand_flags(): flags = within < coverage[:, :, None]  4.86 us
    unnamed x12, local copies, waits for them, and re-layouts  3.92 us
    lt x3, local copies, waits for them, and re-layouts, expand_flags(): flags = within < coverage[:, :, None]  2.96 us
  transfers between devices with their start and end apart: 2, of which 2 were waited for; matrix products, arithmetic and copies ran while one was open for 11% of the time, Pallas kernels for 0%

commit v1 on v0

v1 whole, which is shorter than its diff:
```python
import functools

import jax
import jax.numpy as jnp
from jax import lax
from jax.experimental import pallas as pl
from jax.experimental.pallas import tpu as pltpu
from jax.sharding import PartitionSpec as P

SEG = 128
MESH = pl.DeviceIdType.MESH


def kernel(
    n_epoch, n_tile, images, coverage, scale_out, sky_out,
    held, left, right, power, stage, own, up, down,
    cov_pad, cov_turn, cov_held, cov_rows, cov_cols, inter,
    img_send, img_recv, pass_send, relay_send, relay_recv, cov_send, cov_recv,
    row_send, row_recv, col_send, col_recv, up_send, up_recv, down_send, down_recv,
):
    rows, pixels = images.shape
    segs = pixels // SEG
    n_chip = n_epoch // 2
    blocks = own.shape[0]
    relay = n_chip == 4
    me = lax.axis_index("epoch")
    z = lax.axis_index("tile")
    chip, core = me // 2, me % 2
    sibling = chip * 2 + (1 - core)

    def partner(d):
        other, bit = 0, 1
        while bit < n_chip:
            other = other + ((chip // bit + d // bit) % 2) * bit
            bit *= 2
        return other

    def to_epoch(src, dst, send, recv, target):
        return pltpu.make_async_remote_copy(
            src_ref=src, dst_ref=dst, send_sem=send, recv_sem=recv,
            device_id={"epoch": target}, device_id_type=MESH,
        )

    def to_tile(src, dst, send, recv, target):
        return pltpu.make_async_remote_copy(
            src_ref=src, dst_ref=dst, send_sem=send, recv_sem=recv,
            device_id={"tile": target}, device_id_type=MESH,
        )

    barrier = pltpu.get_barrier_semaphore()
    for d in range(1, n_epoch):
        pl.semaphore_signal(
            barrier, inc=1, device_id={"epoch": (me + d) % n_epoch}, device_id_type=MESH
        )
    for d in range(1, n_tile):
        pl.semaphore_signal(
            barrier, inc=1, device_id={"tile": (z + d) % n_tile}, device_id_type=MESH
        )
    cov_pad[...] = jnp.zeros_like(cov_pad)
    cov_turn[...] = jnp.zeros_like(cov_turn)
    cov_pad[:, :segs] = coverage[...].astype(jnp.float32)
    cov_held[me] = cov_pad[...].T[:segs]
    cov_rows[z] = cov_held[me]
    pl.semaphore_wait(barrier, n_epoch + n_tile - 2)

    cov_copies = []
    for d in range(1, n_epoch):
        cov_copies.append(to_epoch(
            cov_held.at[me], cov_held.at[me], cov_send.at[d - 1], cov_recv.at[me],
            (me + d) % n_epoch,
        ))
    img_copies = []
    direct = [d for d in range(1, n_chip) if not (relay and d == 3)]
    img_copies.append(to_epoch(
        images, held.at[me], img_send.at[0], img_recv.at[me], sibling
    ))
    for d in direct:
        img_copies.append(to_epoch(
            images, held.at[me], img_send.at[d], img_recv.at[me], partner(d) * 2 + core
        ))
    row_copies = []
    for d in range(1, n_tile):
        row_copies.append(to_tile(
            cov_rows.at[z], cov_rows.at[z], row_send.at[d - 1], row_recv.at[z],
            (z + d) % n_tile,
        ))
    for copy in cov_copies + img_copies + row_copies:
        copy.start()

    def image_block(block):
        return to_epoch(
            held.at[block], held.at[block], pass_send.at[0], img_recv.at[block], sibling
        )

    def hand_over(d):
        block = partner(d) * 2 + core
        return to_epoch(
            held.at[block], held.at[block], pass_send.at[d], img_recv.at[block], sibling
        )

    half = rows // 2

    def relay_copy(d):
        block = partner(d) * 2 + core
        part = held.at[block, pl.ds((d - 1) * half, half)]
        return to_epoch(
            part, part, relay_send.at[d - 1], relay_recv.at[d - 1],
            partner(3 - d) * 2 + core,
        )

    def relay_arrived(d):
        block = partner(3) * 2 + core
        part = held.at[block, pl.ds((d - 1) * half, half)]
        return to_epoch(
            part, part, relay_send.at[d - 1], relay_recv.at[d - 1],
            partner(3 - d) * 2 + core,
        )

    lane = lax.broadcasted_iota(jnp.int32, (rows, SEG), 1).astype(jnp.float32)
    for s in range(segs):
        cols = slice(s * SEG, (s + 1) * SEG)
        flag = lane < cov_pad[:, s:s + 1]
        image = images[:, cols]
        held[me, :, cols] = image
        left[:rows, cols] = jnp.where(flag, image.astype(jnp.float32), 0.0).astype(jnp.bfloat16)
        left[rows:, cols] = jnp.where(flag, 1.0, 0.0).astype(jnp.bfloat16)

    def contract(a, b):
        return lax.dot_general(
            a, b, (((1,), (1,)), ((), ())), preferred_element_type=jnp.float32
        )

    parity = (chip % 2 + (chip // 2) % 2) % 2

    def step(n, carry):
        pair = n // 2
        d = jnp.where(
            (parity == 0) & (pair > 0), 1 + pair % (n_chip - 1), pair
        ) if relay else pair
        block = partner(d) * 2 + (core + n) % 2

        @pl.when(n == 2)
        def _():
            for e in direct:
                image_block(partner(e) * 2 + core).wait_recv()
                hand_over(e).start()
                if relay:
                    relay_copy(e).start()

        if relay:
            @pl.when((d == 3) & (n % 2 == 0))
            def _():
                relay_arrived(1).wait_recv()
                relay_arrived(2).wait_recv()
                hand_over(3).start()

        @pl.when(n % 2 == 1)
        def _():
            image_block(block).wait_recv()

        @pl.when(n == 1)
        def _():
            for e in range(1, n_epoch):
                other = (me + e) % n_epoch
                to_epoch(
                    cov_held.at[other], cov_held.at[other], cov_send.at[0],
                    cov_recv.at[other], other,
                ).wait_recv()
            for e in range(1, n_tile):
                target = (z + e) % n_tile
                for j in range(blocks):
                    to_tile(
                        cov_held.at[target * blocks + j], cov_cols.at[z, j],
                        col_send.at[e - 1, j], col_recv.at[z, j], target,
                    ).start()
            for j in range(blocks):
                cov_cols[z, j] = cov_held[z * blocks + j]

        cov_turn[:segs] = cov_held[block]
        cov_pad[...] = cov_turn[...].T
        for s in range(segs):
            cols = slice(s * SEG, (s + 1) * SEG)
            flag = lane < cov_pad[:, s:s + 1]
            masked = jnp.where(flag, held[block, :, cols].astype(jnp.float32), 0.0)
            right[:rows, cols] = masked.astype(jnp.bfloat16)
            right[rows:, cols] = jnp.where(flag, 1.0, 0.0).astype(jnp.bfloat16)
            power[:, cols] = (masked * masked).astype(jnp.bfloat16)

        sums = contract(left[...], right[...])
        stage[0] = sums[:rows, :rows]
        stage[1] = sums[:rows, rows:]
        stage[2] = sums[rows:, :rows]
        stage[3] = contract(left[rows:, :], power[...])

        target = block // blocks

        @pl.when(z == target)
        def _():
            own[block % blocks] = stage[...]

        @pl.when(z < target)
        def _():
            copy = to_tile(
                up.at[block], up.at[block], up_send.at[block], up_recv.at[block],
                jnp.minimum(z + 1, n_tile - 1),
            )

            @pl.when(z == 0)
            def _():
                up[block] = stage[...]

            @pl.when(z > 0)
            def _():
                copy.wait_recv()
                up[block] = up[block] + stage[...]

            copy.start()

        @pl.when(z > target)
        def _():
            copy = to_tile(
                down.at[block], down.at[block], down_send.at[block], down_recv.at[block],
                jnp.maximum(z - 1, 0),
            )

            @pl.when(z == n_tile - 1)
            def _():
                down[block] = stage[...]

            @pl.when(z < n_tile - 1)
            def _():
                copy.wait_recv()
                down[block] = down[block] + stage[...]

            copy.start()

        return carry

    lax.fori_loop(0, n_epoch, step, 0)

    for e in range(1, n_tile):
        other = (z + e) % n_tile
        to_tile(
            cov_rows.at[other], cov_rows.at[other], row_send.at[0], row_recv.at[other], other
        ).wait_recv()
        for j in range(blocks):
            to_tile(
                cov_cols.at[other, j], cov_cols.at[other, j], col_send.at[0, j],
                col_recv.at[other, j], other,
            ).wait_recv()
    inter[...] = jnp.zeros_like(inter)

    def overlap(t, carry):
        cov_turn[:segs] = cov_rows[t]
        cov_pad[...] = cov_turn[...].T
        for j in range(blocks):
            cols = slice(j * rows, (j + 1) * rows)
            total = inter[:, cols]
            for s in range(segs):
                total = total + jnp.minimum(cov_pad[:, s:s + 1], cov_cols[t, j, s:s + 1, :])
            inter[:, cols] = total
        return carry

    lax.fori_loop(0, n_tile, overlap, 0)

    for j in range(blocks):
        block = z * blocks + j

        @pl.when(z > 0)
        def _():
            to_tile(
                up.at[block], up.at[block], up_send.at[block], up_recv.at[block],
                jnp.maximum(z - 1, 0),
            ).wait_recv()
            own[j] = own[j] + up[block]

        @pl.when(z < n_tile - 1)
        def _():
            to_tile(
                down.at[block], down.at[block], down_send.at[block], down_recv.at[block],
                jnp.minimum(z + 1, n_tile - 1),
            ).wait_recv()
            own[j] = own[j] + down[block]

        cols = slice(j * rows, (j + 1) * rows)
        intersection = inter[:, cols]
        cross, flux_i, flux_j, power_j = own[j, 0], own[j, 1], own[j, 2], own[j, 3]
        spread = intersection * power_j - flux_j * flux_j
        covariance = intersection * cross - flux_i * flux_j
        scale_ratio = covariance / (spread + intersection + 1.0)
        scale_out[:, cols] = scale_ratio
        sky_out[:, cols] = (flux_i - scale_ratio * flux_j) / (intersection + 1.0)

    for copy in cov_copies + img_copies + row_copies:
        copy.wait_send()
    for d in range(1, n_chip):
        hand_over(d).wait_send()
    if relay:
        relay_copy(1).wait_send()
        relay_copy(2).wait_send()
    for e in range(1, n_tile):
        target = (z + e) % n_tile
        for j in range(blocks):
            to_tile(
                cov_held.at[target * blocks + j], cov_cols.at[z, j],
                col_send.at[e - 1, j], col_recv.at[z, j], target,
            ).wait_send()

    def drain(block, carry):
        target = block // blocks

        @pl.when(z < target)
        def _():
            to_tile(
                up.at[block], up.at[block], up_send.at[block], up_recv.at[block],
                jnp.minimum(z + 1, n_tile - 1),
            ).wait_send()

        @pl.when(z > target)
        def _():
            to_tile(
                down.at[block], down.at[block], down_send.at[block], down_recv.at[block],
                jnp.maximum(z - 1, 0),
            ).wait_send()

        return carry

    lax.fori_loop(0, n_epoch, drain, 0)


def solution(mesh):
    n_epoch, n_tile = mesh.shape["epoch"], mesh.shape["tile"]

    def body(images, coverage):
        rows, pixels = images.shape
        segs = coverage.shape[1]
        width = rows * n_epoch // n_tile
        blocks = width // rows
        dma, f32 = pltpu.SemaphoreType.DMA, jnp.float32
        out = jax.ShapeDtypeStruct((rows, width), f32)
        vmem = pl.BlockSpec(memory_space=pltpu.VMEM)
        return pl.pallas_call(
            functools.partial(kernel, n_epoch, n_tile),
            out_shape=(out, out),
            in_specs=[vmem, vmem],
            out_specs=(vmem, vmem),
            scratch_shapes=[
                pltpu.VMEM((n_epoch, rows, pixels), jnp.bfloat16),
                pltpu.VMEM((2 * rows, pixels), jnp.bfloat16),
                pltpu.VMEM((2 * rows, pixels), jnp.bfloat16),
                pltpu.VMEM((rows, pixels), jnp.bfloat16),
                pltpu.VMEM((4, rows, rows), f32),
                pltpu.VMEM((blocks, 4, rows, rows), f32),
                pltpu.VMEM((n_epoch, 4, rows, rows), f32),
                pltpu.VMEM((n_epoch, 4, rows, rows), f32),
                pltpu.VMEM((rows, SEG), f32),
                pltpu.VMEM((SEG, rows), f32),
                pltpu.VMEM((n_epoch, segs, rows), f32),
                pltpu.VMEM((n_tile, segs, rows), f32),
                pltpu.VMEM((n_tile, blocks, segs, rows), f32),
                pltpu.VMEM((rows, width), f32),
                dma((n_epoch // 2,)), dma((n_epoch,)), dma((n_epoch // 2,)),
                dma((2,)), dma((2,)), dma((n_epoch,)), dma((n_epoch,)),
                dma((n_tile,)), dma((n_tile,)),
                dma((n_tile, blocks)), dma((n_tile, blocks)),
                dma((n_epoch,)), dma((n_epoch,)), dma((n_epoch,)), dma((n_epoch,)),
            ],
            compiler_params=pltpu.CompilerParams(
                collective_id=0, has_side_effects=True, vmem_limit_bytes=48 * 1024 * 1024
            ),
        )(images, coverage)

    specs = (P("epoch", "tile"), P("epoch", "tile"))
    return jax.shard_map(body, mesh=mesh, in_specs=specs, out_specs=specs, check_vma=False)
```

time: 120 us -> 68.6 us (0.57)
  the two profiles are of different devices: /device:TPU:0 before, /device:TPU:8 now
where the time goes in v1:
time: 68.6 us; the launch traced here: 68.4 us
  Pallas kernels  64.6 us (94%)
  local copies, waits for them, and re-layouts  3.15 us (5%)
    pallas_call x1, Pallas kernels, body(): pl.pallas_call(functools.partial(kernel, n_epoch, n_tile), out_shape=(out...  64.6 us
    unnamed x5, local copies, waits for them, and re-layouts  3.15 us

profile of v1, /device:TPU:8, one launch (start us, length us, event | category | flops | bytes accessed | tf_op | source)
XLA Modules:
  0.0 68.4 jit_solution(15036270786098306599)
XLA Ops:
  0.6 0.8 %copy.4.coverage = s32[128,16]{1,0:T(8,128)S(1)} copy(s32[128,16]{0,1:T(8,128)} %param.3) | data formatting | bytes 16384 | tf_op args[1]
  1.4 0.0 copy-start
  1.4 1.0 %copy-done = bf16[128,2048]{1,0:T(8,128)(2,1)S(1)} copy-done((bf16[128,2048]{1,0:T(8,128)(2,1)S(1)}, bf16[128,2048]{1,0:T(8,128)(2,1)}, u32[]{:S(2)}) %copy-start) | copy-done | bytes 524312
  2.5 64.6 %shard_map.41 = (f32[128,256]{1,0:T(8,128)S(1)}, f32[128,256]{1,0:T(8,128)S(1)}) custom-call(bf16[128,2048]{1,0:T(8,128)(2,1)S(1)} %copy-done, s32[128,16]{1,0:T(8,128)S(1)} %copy.4.coverage), custom_call_target="tpu_custom_call" | custom-call | tf_op jit(solution)/shard_map/pallas_call | solution.py:342
  67.1 0.7 copy.7
  67.7 0.7 copy.8
Async XLA Ops:
  1.4 1.0 %copy-start = (bf16[128,2048]{1,0:T(8,128)(2,1)S(1)}, bf16[128,2048]{1,0:T(8,128)(2,1)}, u32[]{:S(2)}) copy-start(bf16[128,2048]{1,0:T(8,128)(2,1)} %images.1) | copy-start | bytes 1572868

commit v2 on v1

v2 whole, which is shorter than its diff:
```python
import functools

import jax
import jax.numpy as jnp
from jax import lax
from jax.experimental import pallas as pl
from jax.experimental.pallas import tpu as pltpu
from jax.sharding import PartitionSpec as P

SEG = 128
MESH = pl.DeviceIdType.MESH


def kernel(
    n_epoch, n_tile, images, coverage, scale_out, sky_out,
    held, left, right, power, parts, own, up, down,
    cov_pad, cov_turn, cov_held, cov_rows, cov_cols, inter,
    local_sem, img_send, img_recv, pass_send, relay_send, relay_recv, cov_send, cov_recv,
    row_send, row_recv, col_send, col_recv, up_send, up_recv, down_send, down_recv,
):
    rows, pixels = images.shape
    segs = pixels // SEG
    n_chip = n_epoch // 2
    blocks = own.shape[0]
    relay = n_chip == 4
    me = lax.axis_index("epoch")
    z = lax.axis_index("tile")
    chip, core = me // 2, me % 2
    sibling = chip * 2 + (1 - core)

    def partner(d):
        other, bit = 0, 1
        while bit < n_chip:
            other = other + ((chip // bit + d // bit) % 2) * bit
            bit *= 2
        return other

    def to_epoch(src, dst, send, recv, target):
        return pltpu.make_async_remote_copy(
            src_ref=src, dst_ref=dst, send_sem=send, recv_sem=recv,
            device_id={"epoch": target}, device_id_type=MESH,
        )

    def to_tile(src, dst, send, recv, target):
        return pltpu.make_async_remote_copy(
            src_ref=src, dst_ref=dst, send_sem=send, recv_sem=recv,
            device_id={"tile": target}, device_id_type=MESH,
        )

    fetch = pltpu.make_async_copy(images, held.at[me], local_sem)
    fetch.start()
    barrier = pltpu.get_barrier_semaphore()
    for d in range(1, n_epoch):
        pl.semaphore_signal(
            barrier, inc=1, device_id={"epoch": (me + d) % n_epoch}, device_id_type=MESH
        )
    for d in range(1, n_tile):
        pl.semaphore_signal(
            barrier, inc=1, device_id={"tile": (z + d) % n_tile}, device_id_type=MESH
        )
    cov_turn[...] = jnp.zeros_like(cov_turn)
    cov_held[me] = coverage[...].astype(jnp.float32)
    cov_rows[z] = cov_held[me]
    cov_turn[:segs] = cov_held[me]
    cov_pad[...] = cov_turn[...].T
    pl.semaphore_wait(barrier, n_epoch + n_tile - 2)

    cov_copies = []
    for d in range(1, n_epoch):
        cov_copies.append(to_epoch(
            cov_held.at[me], cov_held.at[me], cov_send.at[d - 1], cov_recv.at[me],
            (me + d) % n_epoch,
        ))
    def image_to(d):
        return to_epoch(
            images, held.at[me], img_send.at[d], img_recv.at[me], partner(d) * 2 + core
        )

    to_sibling = to_epoch(images, held.at[me], img_send.at[0], img_recv.at[me], sibling)
    first, second = 1 + core, 2 - core
    start_now = [image_to(first)] if relay else [image_to(d) for d in range(1, n_chip)]
    row_copies = []
    for d in range(1, n_tile):
        row_copies.append(to_tile(
            cov_rows.at[z], cov_rows.at[z], row_send.at[d - 1], row_recv.at[z],
            (z + d) % n_tile,
        ))
    for copy in start_now + [to_sibling] + cov_copies + row_copies:
        copy.start()

    def image_block(block):
        return to_epoch(
            held.at[block], held.at[block], pass_send.at[0], img_recv.at[block], sibling
        )

    def hand_over(d):
        block = partner(d) * 2 + core
        return to_epoch(
            held.at[block], held.at[block], pass_send.at[d], img_recv.at[block], sibling
        )

    half = rows // 2

    def relay_copy(d):
        block = partner(d) * 2 + core
        part = held.at[block, pl.ds(pl.multiple_of((d - 1) * half, half), half)]
        return to_epoch(
            part, part, relay_send.at[d - 1], relay_recv.at[d - 1],
            partner(3 - d) * 2 + core,
        )

    def relay_arrived(d):
        block = partner(3) * 2 + core
        part = held.at[block, pl.ds((d - 1) * half, half)]
        return to_epoch(
            part, part, relay_send.at[d - 1], relay_recv.at[d - 1],
            partner(3 - d) * 2 + core,
        )

    def pass_on(d):
        image_block(partner(d) * 2 + core).wait_recv()
        hand_over(d).start()
        if relay:
            relay_copy(d).start()

    def up_copy(block, i, target):
        ref = up.at[block, i]
        return to_tile(ref, ref, up_send.at[block, i], up_recv.at[block, i], target)

    def down_copy(block, i, target):
        ref = down.at[block, i]
        return to_tile(ref, ref, down_send.at[block, i], down_recv.at[block, i], target)

    above, below = jnp.minimum(z + 1, n_tile - 1), jnp.maximum(z - 1, 0)

    fetch.wait()
    lane = lax.broadcasted_iota(jnp.int32, (rows, SEG), 1).astype(jnp.float32)
    for s in range(segs):
        cols = slice(s * SEG, (s + 1) * SEG)
        flag = lane < cov_pad[:, s:s + 1]
        image = held[me, :, cols]
        left[:rows, cols] = jnp.where(flag, image.astype(jnp.float32), 0.0).astype(jnp.bfloat16)
        left[rows:, cols] = jnp.where(flag, 1.0, 0.0).astype(jnp.bfloat16)

    def contract(a, b):
        return lax.dot_general(
            a, b, (((1,), (1,)), ((), ())), preferred_element_type=jnp.float32
        )

    outer = (chip % 2 + chip // 2) % 2 == 0 if relay else None

    def place(n):
        if not relay:
            return n // 2, (core + n) % 2
        near, late = n % 2, n // 4
        diagonal = jnp.where(outer, n // 2 == 2, n // 2 == 3)
        d = jnp.where(
            late == 0,
            jnp.where(n < 2, 0, jnp.where(near == 0, first, second)),
            jnp.where(diagonal, 3, 2 - near),
        )
        k = jnp.where((late == 0) | diagonal, (core + n) % 2, near)
        return d, k

    def compute(n):
        d, k = place(n)
        block = partner(d) * 2 + k

        @pl.when(n == 2)
        def _():
            if relay:
                pass_on(first)
                image_to(first).wait_send()
                image_to(second).start()
            else:
                for e in range(1, n_chip):
                    pass_on(e)

        if relay:
            @pl.when(n == 4)
            def _():
                pass_on(second)

            @pl.when((d == 3) & (k == core))
            def _():
                relay_arrived(1).wait_recv()
                relay_arrived(2).wait_recv()
                hand_over(3).start()

        @pl.when(k != core)
        def _():
            image_block(block).wait_recv()

        @pl.when(n == 1)
        def _():
            for e in range(1, n_epoch):
                other = (me + e) % n_epoch
                to_epoch(
                    cov_held.at[other], cov_held.at[other], cov_send.at[0],
                    cov_recv.at[other], other,
                ).wait_recv()
            for e in range(1, n_tile):
                target = (z + e) % n_tile
                for j in range(blocks):
                    to_tile(
                        cov_held.at[target * blocks + j], cov_cols.at[z, j],
                        col_send.at[e - 1, j], col_recv.at[z, j], target,
                    ).start()
            for j in range(blocks):
                cov_cols[z, j] = cov_held[z * blocks + j]

        cov_turn[:segs] = cov_held[block]
        cov_pad[...] = cov_turn[...].T
        for s in range(segs):
            cols = slice(s * SEG, (s + 1) * SEG)
            flag = lane < cov_pad[:, s:s + 1]
            masked = jnp.where(flag, held[block, :, cols].astype(jnp.float32), 0.0)
            right[:rows, cols] = masked.astype(jnp.bfloat16)
            right[rows:, cols] = jnp.where(flag, 1.0, 0.0).astype(jnp.bfloat16)
            power[:, cols] = (masked * masked).astype(jnp.bfloat16)

        sums = contract(left[...], right[...])
        parts[block, 0] = sums[:rows, :rows]
        parts[block, 1] = sums[:rows, rows:]
        parts[block, 2] = sums[rows:, :rows]
        parts[block, 3] = contract(left[rows:, :], power[...])

        target = block // blocks

        @pl.when(z == target)
        def _():
            own[block % blocks] = parts[block]

        @pl.when((z == 0) & (target > 0))
        def _():
            up[block] = parts[block]
            for i in range(4):
                up_copy(block, i, above).start()

        @pl.when((z == n_tile - 1) & (target < n_tile - 1))
        def _():
            down[block] = parts[block]
            for i in range(4):
                down_copy(block, i, below).start()

    def forward(n):
        d, k = place(n)
        block = partner(d) * 2 + k
        target = block // blocks

        @pl.when((z > 0) & (z < target))
        def _():
            for i in range(4):
                up_copy(block, i, above).wait_recv()
                up[block, i] = up[block, i] + parts[block, i]
                up_copy(block, i, above).start()

        @pl.when((z < n_tile - 1) & (z > target))
        def _():
            for i in range(4):
                down_copy(block, i, below).wait_recv()
                down[block, i] = down[block, i] + parts[block, i]
                down_copy(block, i, below).start()

    def intersect():
        for e in range(1, n_tile):
            other = (z + e) % n_tile
            to_tile(
                cov_rows.at[other], cov_rows.at[other], row_send.at[0], row_recv.at[other], other
            ).wait_recv()
            for j in range(blocks):
                to_tile(
                    cov_cols.at[other, j], cov_cols.at[other, j], col_send.at[0, j],
                    col_recv.at[other, j], other,
                ).wait_recv()
        inter[...] = jnp.zeros_like(inter)

        def overlap(t, carry):
            cov_turn[:segs] = cov_rows[t]
            cov_pad[...] = cov_turn[...].T
            for j in range(blocks):
                cols = slice(j * rows, (j + 1) * rows)
                total = inter[:, cols]
                for s in range(segs):
                    total = total + jnp.minimum(cov_pad[:, s:s + 1], cov_cols[t, j, s:s + 1, :])
                inter[:, cols] = total
            return carry

        lax.fori_loop(0, n_tile, overlap, 0)

    lag = 2

    def step(n, carry):
        @pl.when(n < n_epoch)
        def _():
            compute(n)

        @pl.when(n == n_epoch - 3)
        def _():
            intersect()

        @pl.when(n >= lag)
        def _():
            forward(n - lag)

        return carry

    lax.fori_loop(0, n_epoch + lag, step, 0)

    for j in range(blocks):
        block = z * blocks + j

        @pl.when(z > 0)
        def _():
            for i in range(4):
                up_copy(block, i, below).wait_recv()
            own[j] = own[j] + up[block]

        @pl.when(z < n_tile - 1)
        def _():
            for i in range(4):
                down_copy(block, i, above).wait_recv()
            own[j] = own[j] + down[block]

        cols = slice(j * rows, (j + 1) * rows)
        intersection = inter[:, cols]
        cross, flux_i, flux_j, power_j = own[j, 0], own[j, 1], own[j, 2], own[j, 3]
        spread = intersection * power_j - flux_j * flux_j
        covariance = intersection * cross - flux_i * flux_j
        scale_ratio = covariance / (spread + intersection + 1.0)
        scale_out[:, cols] = scale_ratio
        sky_out[:, cols] = (flux_i - scale_ratio * flux_j) / (intersection + 1.0)

    late = [image_to(second)] if relay else start_now
    for copy in late + [to_sibling] + cov_copies + row_copies:
        copy.wait_send()
    for d in range(1, n_chip):
        hand_over(d).wait_send()
    if relay:
        relay_copy(1).wait_send()
        relay_copy(2).wait_send()
    for e in range(1, n_tile):
        target = (z + e) % n_tile
        for j in range(blocks):
            to_tile(
                cov_held.at[target * blocks + j], cov_cols.at[z, j],
                col_send.at[e - 1, j], col_recv.at[z, j], target,
            ).wait_send()

    def drain(block, carry):
        target = block // blocks

        @pl.when(z < target)
        def _():
            for i in range(4):
                up_copy(block, i, above).wait_send()

        @pl.when(z > target)
        def _():
            for i in range(4):
                down_copy(block, i, below).wait_send()

        return carry

    lax.fori_loop(0, n_epoch, drain, 0)


def solution(mesh):
    n_epoch, n_tile = mesh.shape["epoch"], mesh.shape["tile"]

    def body(images, coverage):
        rows, pixels = images.shape
        segs = coverage.shape[1]
        width = rows * n_epoch // n_tile
        blocks = width // rows
        dma, f32 = pltpu.SemaphoreType.DMA, jnp.float32
        out = jax.ShapeDtypeStruct((rows, width), f32)
        vmem = pl.BlockSpec(memory_space=pltpu.VMEM)
        return pl.pallas_call(
            functools.partial(kernel, n_epoch, n_tile),
            out_shape=(out, out),
            in_specs=[pl.BlockSpec(memory_space=pltpu.HBM), vmem],
            out_specs=(vmem, vmem),
            scratch_shapes=[
                pltpu.VMEM((n_epoch, rows, pixels), jnp.bfloat16),
                pltpu.VMEM((2 * rows, pixels), jnp.bfloat16),
                pltpu.VMEM((2 * rows, pixels), jnp.bfloat16),
                pltpu.VMEM((rows, pixels), jnp.bfloat16),
                pltpu.VMEM((n_epoch, 4, rows, rows), f32),
                pltpu.VMEM((blocks, 4, rows, rows), f32),
                pltpu.VMEM((n_epoch, 4, rows, rows), f32),
                pltpu.VMEM((n_epoch, 4, rows, rows), f32),
                pltpu.VMEM((rows, SEG), f32),
                pltpu.VMEM((SEG, rows), f32),
                pltpu.VMEM((n_epoch, segs, rows), f32),
                pltpu.VMEM((n_tile, segs, rows), f32),
                pltpu.VMEM((n_tile, blocks, segs, rows), f32),
                pltpu.VMEM((rows, width), f32),
                dma, dma((n_epoch // 2,)), dma((n_epoch,)), dma((n_epoch // 2,)),
                dma((2,)), dma((2,)), dma((n_epoch,)), dma((n_epoch,)),
                dma((n_tile,)), dma((n_tile,)),
                dma((n_tile, blocks)), dma((n_tile, blocks)),
                dma((n_epoch, 4)), dma((n_epoch, 4)), dma((n_epoch, 4)), dma((n_epoch, 4)),
            ],
            compiler_params=pltpu.CompilerParams(
                collective_id=0, has_side_effects=True, vmem_limit_bytes=48 * 1024 * 1024
            ),
        )(images, coverage.T)

    specs = (P("epoch", "tile"), P("epoch", "tile"))
    return jax.shard_map(body, mesh=mesh, in_specs=specs, out_specs=specs, check_vma=False)
```

time: 68.6 us -> 69.2 us (level)
  the two profiles are of different devices: /device:TPU:8 before, /device:TPU:13 now
where the time goes in v2:
time: 69.2 us; the launch traced here: 69 us
  Pallas kernels  65.3 us (94%)
  local copies, waits for them, and re-layouts  3.04 us (4%)
    pallas_call x1, Pallas kernels, body(): pl.pallas_call(functools.partial(kernel, n_epoch, n_tile), out_shape=(out...  65.3 us
    unnamed x6, local copies, waits for them, and re-layouts  3.04 us

profile of v2, /device:TPU:13, one launch (start us, length us, event | category | flops | bytes accessed | tf_op | source)
XLA Modules:
  0.0 69.0 jit_solution(9133535425019048764)
XLA Ops:
  0.6 0.0 copy-start
  0.6 1.0 %copy-done = bf16[128,2048]{1,0:T(8,128)(2,1)S(1)} copy-done((bf16[128,2048]{1,0:T(8,128)(2,1)S(1)}, bf16[128,2048]{1,0:T(8,128)(2,1)}, u32[]{:S(2)}) %copy-start) | copy-done | bytes 524312
  1.7 0.0 copy-start.1
  1.7 0.7 %copy-done.1 = s32[128,16]{0,1:T(8,128)S(1)} copy-done((s32[128,16]{0,1:T(8,128)S(1)}, s32[128,16]{0,1:T(8,128)}, u32[]{:S(2)}) %copy-start.1) | copy-done | bytes 8216
  2.4 65.3 %shard_map.41 = (f32[128,256]{1,0:T(8,128)S(1)}, f32[128,256]{1,0:T(8,128)S(1)}) custom-call(bf16[128,2048]{1,0:T(8,128)(2,1)S(1)} %copy-done, s32[16,128]{1,0:T(8,128)S(1)} %bitcast.1), custom_call_target="tpu_custom_call" | custom-call | tf_op jit(solution)/shard_map/pallas_call | solution.py:379
  67.7 0.7 copy.6
  68.4 0.7 copy.7
Async XLA Ops:
  0.6 1.0 %copy-start = (bf16[128,2048]{1,0:T(8,128)(2,1)S(1)}, bf16[128,2048]{1,0:T(8,128)(2,1)}, u32[]{:S(2)}) copy-start(bf16[128,2048]{1,0:T(8,128)(2,1)} %images.1) | copy-start | bytes 1572868
  1.7 0.7 %copy-start.1 = (s32[128,16]{0,1:T(8,128)S(1)}, s32[128,16]{0,1:T(8,128)}, u32[]{:S(2)}) copy-start(s32[128,16]{0,1:T(8,128)} %param.3) | copy-start | bytes 24580

commit v3 on v2

--- a/solution.py
+++ b/solution.py
@@ -13,8 +13,8 @@
 
 def kernel(
     n_epoch, n_tile, images, coverage, scale_out, sky_out,
-    held, left, right, power, parts, own, up, down,
-    cov_pad, cov_turn, cov_held, cov_rows, cov_cols, inter,
+    held, left, right, parts, own, up, down,
+    cov_own, cov_pad, cov_turn, cov_held, cov_rows, cov_cols, inter,
     local_sem, img_send, img_recv, pass_send, relay_send, relay_recv, cov_send, cov_recv,
     row_send, row_recv, col_send, col_recv, up_send, up_recv, down_send, down_recv,
 ):
@@ -47,7 +47,9 @@
             device_id={"tile": target}, device_id_type=MESH,
         )
 
-    fetch = pltpu.make_async_copy(images, held.at[me], local_sem)
+    fetch_cov = pltpu.make_async_copy(coverage, cov_own, local_sem.at[1])
+    fetch_cov.start()
+    fetch = pltpu.make_async_copy(images, held.at[me], local_sem.at[0])
     fetch.start()
     barrier = pltpu.get_barrier_semaphore()
     for d in range(1, n_epoch):
@@ -59,7 +61,8 @@
             barrier, inc=1, device_id={"tile": (z + d) % n_tile}, device_id_type=MESH
         )
     cov_turn[...] = jnp.zeros_like(cov_turn)
-    cov_held[me] = coverage[...].astype(jnp.float32)
+    fetch_cov.wait()
+    cov_held[me] = cov_own[...].astype(jnp.float32)
     cov_rows[z] = cov_held[me]
     cov_turn[:segs] = cov_held[me]
     cov_pad[...] = cov_turn[...].T
@@ -135,17 +138,13 @@
 
     fetch.wait()
     lane = lax.broadcasted_iota(jnp.int32, (rows, SEG), 1).astype(jnp.float32)
+    down_lane = lax.broadcasted_iota(jnp.int32, (SEG, rows), 0).astype(jnp.float32)
     for s in range(segs):
-        cols = slice(s * SEG, (s + 1) * SEG)
-        flag = lane < cov_pad[:, s:s + 1]
-        image = held[me, :, cols]
-        left[:rows, cols] = jnp.where(flag, image.astype(jnp.float32), 0.0).astype(jnp.bfloat16)
-        left[rows:, cols] = jnp.where(flag, 1.0, 0.0).astype(jnp.bfloat16)
-
-    def contract(a, b):
-        return lax.dot_general(
-            a, b, (((1,), (1,)), ((), ())), preferred_element_type=jnp.float32
-        )
+        span = slice(s * SEG, (s + 1) * SEG)
+        flag = down_lane < cov_turn[s:s + 1, :]
+        image = held[me, :, span].astype(jnp.float32).T
+        left[span, :rows] = jnp.where(flag, image, 0.0).astype(jnp.bfloat16)
+        left[span, rows:] = jnp.where(flag, 1.0, 0.0).astype(jnp.bfloat16)
 
     outer = (chip % 2 + chip // 2) % 2 == 0 if relay else None
 
@@ -216,14 +215,14 @@
             flag = lane < cov_pad[:, s:s + 1]
             masked = jnp.where(flag, held[block, :, cols].astype(jnp.float32), 0.0)
             right[:rows, cols] = masked.astype(jnp.bfloat16)
-            right[rows:, cols] = jnp.where(flag, 1.0, 0.0).astype(jnp.bfloat16)
-            power[:, cols] = (masked * masked).astype(jnp.bfloat16)
-
-        sums = contract(left[...], right[...])
+            right[rows:2 * rows, cols] = jnp.where(flag, 1.0, 0.0).astype(jnp.bfloat16)
+            right[2 * rows:, cols] = (masked * masked).astype(jnp.bfloat16)
+
+        sums = jnp.dot(right[...], left[...], preferred_element_type=jnp.float32)
         parts[block, 0] = sums[:rows, :rows]
-        parts[block, 1] = sums[:rows, rows:]
-        parts[block, 2] = sums[rows:, :rows]
-        parts[block, 3] = contract(left[rows:, :], power[...])
+        parts[block, 1] = sums[rows:2 * rows, :rows]
+        parts[block, 2] = sums[:rows, rows:]
+        parts[block, 3] = sums[2 * rows:, rows:]
 
         target = block // blocks
 
@@ -276,14 +275,13 @@
         inter[...] = jnp.zeros_like(inter)
 
         def overlap(t, carry):
-            cov_turn[:segs] = cov_rows[t]
-            cov_pad[...] = cov_turn[...].T
             for j in range(blocks):
-                cols = slice(j * rows, (j + 1) * rows)
-                total = inter[:, cols]
+                cov_turn[:segs] = cov_cols[t, j]
+                cov_pad[...] = cov_turn[...].T
+                total = inter[j]
                 for s in range(segs):
-                    total = total + jnp.minimum(cov_pad[:, s:s + 1], cov_cols[t, j, s:s + 1, :])
-                inter[:, cols] = total
+                    total = total + jnp.minimum(cov_pad[:, s:s + 1], cov_rows[t, s:s + 1, :])
+                inter[j] = total
             return carry
 
         lax.fori_loop(0, n_tile, overlap, 0)
@@ -323,13 +321,13 @@
             own[j] = own[j] + down[block]
 
         cols = slice(j * rows, (j + 1) * rows)
-        intersection = inter[:, cols]
+        intersection = inter[j]
         cross, flux_i, flux_j, power_j = own[j, 0], own[j, 1], own[j, 2], own[j, 3]
         spread = intersection * power_j - flux_j * flux_j
         covariance = intersection * cross - flux_i * flux_j
         scale_ratio = covariance / (spread + intersection + 1.0)
-        scale_out[:, cols] = scale_ratio
-        sky_out[:, cols] = (flux_i - scale_ratio * flux_j) / (intersection + 1.0)
+        scale_out[:, cols] = scale_ratio.T
+        sky_out[:, cols] = ((flux_i - scale_ratio * flux_j) / (intersection + 1.0)).T
 
     late = [image_to(second)] if relay else start_now
     for copy in late + [to_sibling] + cov_copies + row_copies:
@@ -379,31 +377,31 @@
         return pl.pallas_call(
             functools.partial(kernel, n_epoch, n_tile),
             out_shape=(out, out),
-            in_specs=[pl.BlockSpec(memory_space=pltpu.HBM), vmem],
+            in_specs=[pl.BlockSpec(memory_space=pl.ANY)] * 2,
             out_specs=(vmem, vmem),
             scratch_shapes=[
                 pltpu.VMEM((n_epoch, rows, pixels), jnp.bfloat16),
-                pltpu.VMEM((2 * rows, pixels), jnp.bfloat16),
-                pltpu.VMEM((2 * rows, pixels), jnp.bfloat16),
-                pltpu.VMEM((rows, pixels), jnp.bfloat16),
+                pltpu.VMEM((pixels, 2 * rows), jnp.bfloat16),
+                pltpu.VMEM((3 * rows, pixels), jnp.bfloat16),
                 pltpu.VMEM((n_epoch, 4, rows, rows), f32),
                 pltpu.VMEM((blocks, 4, rows, rows), f32),
                 pltpu.VMEM((n_epoch, 4, rows, rows), f32),
                 pltpu.VMEM((n_epoch, 4, rows, rows), f32),
+                pltpu.VMEM((segs, rows), jnp.int32),
                 pltpu.VMEM((rows, SEG), f32),
                 pltpu.VMEM((SEG, rows), f32),
                 pltpu.VMEM((n_epoch, segs, rows), f32),
                 pltpu.VMEM((n_tile, segs, rows), f32),
                 pltpu.VMEM((n_tile, blocks, segs, rows), f32),
-                pltpu.VMEM((rows, width), f32),
-                dma, dma((n_epoch // 2,)), dma((n_epoch,)), dma((n_epoch // 2,)),
+                pltpu.VMEM((blocks, rows, rows), f32),
+                dma((2,)), dma((n_epoch // 2,)), dma((n_epoch,)), dma((n_epoch // 2,)),
                 dma((2,)), dma((2,)), dma((n_epoch,)), dma((n_epoch,)),
                 dma((n_tile,)), dma((n_tile,)),
                 dma((n_tile, blocks)), dma((n_tile, blocks)),
                 dma((n_epoch, 4)), dma((n_epoch, 4)), dma((n_epoch, 4)), dma((n_epoch, 4)),
             ],
             compiler_params=pltpu.CompilerParams(
-                collective_id=0, has_side_effects=True, vmem_limit_bytes=48 * 1024 * 1024
+                collective_id=0, has_side_effects=True, vmem_limit_bytes=62 * 1024 * 1024
             ),
         )(images, coverage.T)
 

time: 69.2 us -> 69.4 us (level)
  Pallas kernels: 65.3 us -> 66.3 us
  local copies, waits for them, and re-layouts: 3.04 us -> 2.26 us
    pallas_call x1, Pallas kernels: 65.3 us -> 66.3 us  [body(): pl.pallas_call(functools.partial(kernel, n_epoch, n_tile), out_shape=(out...]
    unnamed x6 -> x4, local copies, waits for them, and re-layouts: 3.04 us -> 2.26 us
where the time goes in v3:
time: 69.4 us; the launch traced here: 69.2 us
  Pallas kernels  66.3 us (96%)
  local copies, waits for them, and re-layouts  2.26 us (3%)
    pallas_call x1, Pallas kernels, body(): pl.pallas_call(functools.partial(kernel, n_epoch, n_tile), out_shape=(out...  66.3 us
    unnamed x4, local copies, waits for them, and re-layouts  2.26 us

profile of v3, /device:TPU:13, one launch (start us, length us, event | category | flops | bytes accessed | tf_op | source)
XLA Modules:
  0.0 69.2 jit_solution(355079647975510190)
XLA Ops:
  0.6 66.3 %shard_map.41 = (f32[128,256]{1,0:T(8,128)}, f32[128,256]{1,0:T(8,128)}) custom-call(bf16[128,2048]{1,0:T(8,128)(2,1)} %images.1, s32[16,128]{1,0:T(8,128)} %bitcast.1), custom_call_target="tpu_custom_call" | custom-call | tf_op jit(solution)/shard_map/pallas_call | solution.py:377
  66.9 0.0 copy-start
  66.9 1.6 %copy.6 = f32[128,256]{1,0:T(8,128)} copy(f32[128,256]{1,0:T(8,128)} %get-tuple-element.4) | data formatting | bytes 262144
  68.5 0.0 copy-done
  68.5 0.7 copy.7
Async XLA Ops:
  66.9 1.6 %copy-start = (f32[128,256]{1,0:T(8,128)S(1)}, f32[128,256]{1,0:T(8,128)}, u32[]{:S(2)}) copy-start(f32[128,256]{1,0:T(8,128)} %get-tuple-element.5) | copy-start | bytes 393220

commit v4 on v3

--- a/solution.py
+++ b/solution.py
@@ -148,11 +148,13 @@
 
     outer = (chip % 2 + chip // 2) % 2 == 0 if relay else None
 
-    def place(n):
+    end = (z == 0) | (z == n_tile - 1)
+
+    def place(n, early):
         if not relay:
             return n // 2, (core + n) % 2
         near, late = n % 2, n // 4
-        diagonal = jnp.where(outer, n // 2 == 2, n // 2 == 3)
+        diagonal = n // 2 == jnp.where(early, 2, 3)
         d = jnp.where(
             late == 0,
             jnp.where(n < 2, 0, jnp.where(near == 0, first, second)),
@@ -162,7 +164,7 @@
         return d, k
 
     def compute(n):
-        d, k = place(n)
+        d, k = place(n, outer & end if relay else None)
         block = partner(d) * 2 + k
 
         @pl.when(n == 2)
@@ -243,7 +245,7 @@
                 down_copy(block, i, below).start()
 
     def forward(n):
-        d, k = place(n)
+        d, k = place(n, outer)
         block = partner(d) * 2 + k
         target = block // blocks
 
@@ -286,7 +288,7 @@
 
         lax.fori_loop(0, n_tile, overlap, 0)
 
-    lag = 2
+    lag = 4
 
     def step(n, carry):
         @pl.when(n < n_epoch)

time: 69.4 us -> 74.7 us (1.076)
  the two profiles are of different devices: /device:TPU:13 before, /device:TPU:12 now
where the time goes in v4:
time: 74.7 us; the launch traced here: 74.5 us
  Pallas kernels  71.6 us (96%)
  local copies, waits for them, and re-layouts  2.26 us (3%)
    pallas_call x1, Pallas kernels, body(): pl.pallas_call(functools.partial(kernel, n_epoch, n_tile), out_shape=(out...  71.6 us
    unnamed x4, local copies, waits for them, and re-layouts  2.26 us

profile of v4, /device:TPU:12, one launch (start us, length us, event | category | flops | bytes accessed | tf_op | source)
XLA Modules:
  0.0 74.5 jit_solution(17009682716222185874)
XLA Ops:
  0.6 71.6 %shard_map.41 = (f32[128,256]{1,0:T(8,128)}, f32[128,256]{1,0:T(8,128)}) custom-call(bf16[128,2048]{1,0:T(8,128)(2,1)} %images.1, s32[16,128]{1,0:T(8,128)} %bitcast.1), custom_call_target="tpu_custom_call" | custom-call | tf_op jit(solution)/shard_map/pallas_call | solution.py:379
  72.2 0.0 copy-start
  72.2 1.6 %copy.6 = f32[128,256]{1,0:T(8,128)} copy(f32[128,256]{1,0:T(8,128)} %get-tuple-element.4) | data formatting | bytes 262144
  73.8 0.0 copy-done
  73.9 0.7 copy.7
Async XLA Ops:
  72.2 1.6 %copy-start = (f32[128,256]{1,0:T(8,128)S(1)}, f32[128,256]{1,0:T(8,128)}, u32[]{:S(2)}) copy-start(f32[128,256]{1,0:T(8,128)} %get-tuple-element.5) | copy-start | bytes 393220

commit v5 on v3

--- a/solution.py
+++ b/solution.py
@@ -14,7 +14,7 @@
 def kernel(
     n_epoch, n_tile, images, coverage, scale_out, sky_out,
     held, left, right, parts, own, up, down,
-    cov_own, cov_pad, cov_turn, cov_held, cov_rows, cov_cols, inter,
+    cov_own, cov_turn, meet_turn, spread_out, cov_held, cov_rows, cov_cols, inter,
     local_sem, img_send, img_recv, pass_send, relay_send, relay_recv, cov_send, cov_recv,
     row_send, row_recv, col_send, col_recv, up_send, up_recv, down_send, down_recv,
 ):
@@ -64,8 +64,16 @@
     fetch_cov.wait()
     cov_held[me] = cov_own[...].astype(jnp.float32)
     cov_rows[z] = cov_held[me]
+    pixel = lax.broadcasted_iota(jnp.int32, (SEG, pixels), 1)
+    line = lax.broadcasted_iota(jnp.int32, (SEG, pixels), 0)
+    spread_out[...] = jnp.where(
+        line == segs, -(pixel % SEG), jnp.where(line == pixel // SEG, 1, 0)
+    ).astype(jnp.float32).astype(jnp.bfloat16)
+    cov_turn[segs:segs + 8] = jnp.where(
+        lax.broadcasted_iota(jnp.int32, (8, rows), 0) == 0, 1.0, 0.0
+    )
+    meet_turn[...] = jnp.zeros_like(meet_turn)
     cov_turn[:segs] = cov_held[me]
-    cov_pad[...] = cov_turn[...].T
     pl.semaphore_wait(barrier, n_epoch + n_tile - 2)
 
     cov_copies = []
@@ -137,7 +145,6 @@
     above, below = jnp.minimum(z + 1, n_tile - 1), jnp.maximum(z - 1, 0)
 
     fetch.wait()
-    lane = lax.broadcasted_iota(jnp.int32, (rows, SEG), 1).astype(jnp.float32)
     down_lane = lax.broadcasted_iota(jnp.int32, (SEG, rows), 0).astype(jnp.float32)
     for s in range(segs):
         span = slice(s * SEG, (s + 1) * SEG)
@@ -209,14 +216,16 @@
                 cov_cols[z, j] = cov_held[z * blocks + j]
 
         cov_turn[:segs] = cov_held[block]
-        cov_pad[...] = cov_turn[...].T
-        for s in range(segs):
-            cols = slice(s * SEG, (s + 1) * SEG)
-            flag = lane < cov_pad[:, s:s + 1]
-            masked = jnp.where(flag, held[block, :, cols].astype(jnp.float32), 0.0)
-            right[:rows, cols] = masked.astype(jnp.bfloat16)
-            right[rows:2 * rows, cols] = jnp.where(flag, 1.0, 0.0).astype(jnp.bfloat16)
-            right[2 * rows:, cols] = (masked * masked).astype(jnp.bfloat16)
+        left_over = jnp.dot(
+            cov_turn[...].T.astype(jnp.bfloat16), spread_out[...],
+            preferred_element_type=jnp.float32,
+        )
+        flags = jnp.clip(left_over, 0.0, 1.0).astype(jnp.bfloat16)
+        masked = held[block] * flags
+        right[:rows] = masked
+        right[rows:2 * rows] = flags
+        wide = masked.astype(jnp.float32)
+        right[2 * rows:] = (wide * wide).astype(jnp.bfloat16)
 
         sums = jnp.dot(right[...], left[...], preferred_element_type=jnp.float32)
         parts[block, 0] = sums[:rows, :rows]
@@ -276,11 +285,16 @@
 
         def overlap(t, carry):
             for j in range(blocks):
-                cov_turn[:segs] = cov_cols[t, j]
-                cov_pad[...] = cov_turn[...].T
+                meet_turn[:segs] = cov_cols[t, j]
+                across = jnp.dot(
+                    meet_turn[...].T.astype(jnp.bfloat16), spread_out[...],
+                    preferred_element_type=jnp.float32,
+                )
                 total = inter[j]
                 for s in range(segs):
-                    total = total + jnp.minimum(cov_pad[:, s:s + 1], cov_rows[t, s:s + 1, :])
+                    total = total + jnp.minimum(
+                        across[:, s * SEG:s * SEG + rows], cov_rows[t, s:s + 1, :]
+                    )
                 inter[j] = total
             return carry
 
@@ -388,8 +402,9 @@
                 pltpu.VMEM((n_epoch, 4, rows, rows), f32),
                 pltpu.VMEM((n_epoch, 4, rows, rows), f32),
                 pltpu.VMEM((segs, rows), jnp.int32),
-                pltpu.VMEM((rows, SEG), f32),
                 pltpu.VMEM((SEG, rows), f32),
+                pltpu.VMEM((SEG, rows), f32),
+                pltpu.VMEM((SEG, pixels), jnp.bfloat16),
                 pltpu.VMEM((n_epoch, segs, rows), f32),
                 pltpu.VMEM((n_tile, segs, rows), f32),
                 pltpu.VMEM((n_tile, blocks, segs, rows), f32),

time: 69.4 us -> 67.6 us (0.974)
  Pallas kernels: 66.3 us -> 64.5 us
    pallas_call x1, Pallas kernels: 66.3 us -> 64.5 us  [body(): pl.pallas_call(functools.partial(kernel, n_epoch, n_tile), out_shape=(out...]
where the time goes in v5:
time: 67.6 us; the launch traced here: 67.4 us
  Pallas kernels  64.5 us (95%)
  local copies, waits for them, and re-layouts  2.26 us (3%)
    pallas_call x1, Pallas kernels, body(): pl.pallas_call(functools.partial(kernel, n_epoch, n_tile), out_shape=(out...  64.5 us
    unnamed x4, local copies, waits for them, and re-layouts  2.26 us

profile of v5, /device:TPU:13, one launch (start us, length us, event | category | flops | bytes accessed | tf_op | source)
XLA Modules:
  0.0 67.4 jit_solution(6673340982390209579)
XLA Ops:
  0.6 64.5 %shard_map.41 = (f32[128,256]{1,0:T(8,128)}, f32[128,256]{1,0:T(8,128)}) custom-call(bf16[128,2048]{1,0:T(8,128)(2,1)} %images.1, s32[16,128]{1,0:T(8,128)} %bitcast.1), custom_call_target="tpu_custom_call" | custom-call | tf_op jit(solution)/shard_map/pallas_call | solution.py:391
  65.1 0.0 copy-start
  65.1 1.6 %copy.6 = f32[128,256]{1,0:T(8,128)} copy(f32[128,256]{1,0:T(8,128)} %get-tuple-element.4) | data formatting | bytes 262144
  66.7 0.0 copy-done
  66.7 0.7 copy.7
Async XLA Ops:
  65.1 1.6 %copy-start = (f32[128,256]{1,0:T(8,128)S(1)}, f32[128,256]{1,0:T(8,128)}, u32[]{:S(2)}) copy-start(f32[128,256]{1,0:T(8,128)} %get-tuple-element.5) | copy-start | bytes 393220

commit v6 on v5

--- a/solution.py
+++ b/solution.py
@@ -252,6 +252,13 @@
                 down_copy(block, i, below).start()
 
     def forward(n):
+        if relay:
+            even = n - n % 2
+            d, k = place(even)
+            rising = jnp.where((partner(d) * 2 + k) // blocks > z, 1, 0)
+            wanted = jnp.where(z < n_tile // 2, 1, 0)
+            swap = (~outer) & (n >= 2) & (n < 6) & (rising != wanted)
+            n = jnp.where(swap, even + 1 - n % 2, n)
         d, k = place(n)
         block = partner(d) * 2 + k
         target = block // blocks

time: 67.6 us -> 62.3 us (0.922)
  the two profiles are of different devices: /device:TPU:13 before, /device:TPU:8 now
where the time goes in v6:
time: 62.3 us; the launch traced here: 62.1 us
  Pallas kernels  59.2 us (95%)
  local copies, waits for them, and re-layouts  2.26 us (4%)
  between operations  0.65 us (1%)
    pallas_call x1, Pallas kernels, body(): pl.pallas_call(functools.partial(kernel, n_epoch, n_tile), out_shape=(out...  59.2 us
    unnamed x4, local copies, waits for them, and re-layouts  2.26 us

profile of v6, /device:TPU:8, one launch (start us, length us, event | category | flops | bytes accessed | tf_op | source)
XLA Modules:
  0.0 62.1 jit_solution(2178709659268947864)
XLA Ops:
  0.6 59.2 %shard_map.41 = (f32[128,256]{1,0:T(8,128)}, f32[128,256]{1,0:T(8,128)}) custom-call(bf16[128,2048]{1,0:T(8,128)(2,1)} %images.1, s32[16,128]{1,0:T(8,128)} %bitcast.1), custom_call_target="tpu_custom_call" | custom-call | tf_op jit(solution)/shard_map/pallas_call | solution.py:398
  59.9 0.0 copy-start
  59.9 1.6 %copy.6 = f32[128,256]{1,0:T(8,128)} copy(f32[128,256]{1,0:T(8,128)} %get-tuple-element.4) | data formatting | bytes 262144
  61.5 0.0 copy-done
  61.5 0.7 %copy.7 = f32[128,256]{1,0:T(8,128)} copy(f32[128,256]{1,0:T(8,128)S(1)} %copy-done) | data formatting | bytes 262144
Async XLA Ops:
  59.9 1.6 %copy-start = (f32[128,256]{1,0:T(8,128)S(1)}, f32[128,256]{1,0:T(8,128)}, u32[]{:S(2)}) copy-start(f32[128,256]{1,0:T(8,128)} %get-tuple-element.5) | copy-start | bytes 393220

commit v7 on v6

--- a/solution.py
+++ b/solution.py
@@ -60,10 +60,39 @@
         pl.semaphore_signal(
             barrier, inc=1, device_id={"tile": (z + d) % n_tile}, device_id_type=MESH
         )
+    pl.semaphore_wait(barrier, n_epoch + n_tile - 2)
+
+    def image_to(d):
+        return to_epoch(
+            images, held.at[me], img_send.at[d], img_recv.at[me], partner(d) * 2 + core
+        )
+
+    to_sibling = to_epoch(images, held.at[me], img_send.at[0], img_recv.at[me], sibling)
+    first, second = 1 + core, 2 - core
+    start_now = [image_to(first)] if relay else [image_to(d) for d in range(1, n_chip)]
+    for copy in start_now + [to_sibling]:
+        copy.start()
+
     cov_turn[...] = jnp.zeros_like(cov_turn)
     fetch_cov.wait()
     cov_held[me] = cov_own[...].astype(jnp.float32)
     cov_rows[z] = cov_held[me]
+
+    cov_copies = []
+    for d in range(1, n_epoch):
+        cov_copies.append(to_epoch(
+            cov_held.at[me], cov_held.at[me], cov_send.at[d - 1], cov_recv.at[me],
+            (me + d) % n_epoch,
+        ))
+    row_copies = []
+    for d in range(1, n_tile):
+        row_copies.append(to_tile(
+            cov_rows.at[z], cov_rows.at[z], row_send.at[d - 1], row_recv.at[z],
+            (z + d) % n_tile,
+        ))
+    for copy in cov_copies + row_copies:
+        copy.start()
+
     pixel = lax.broadcasted_iota(jnp.int32, (SEG, pixels), 1)
     line = lax.broadcasted_iota(jnp.int32, (SEG, pixels), 0)
     spread_out[...] = jnp.where(
@@ -74,30 +103,6 @@
     )
     meet_turn[...] = jnp.zeros_like(meet_turn)
     cov_turn[:segs] = cov_held[me]
-    pl.semaphore_wait(barrier, n_epoch + n_tile - 2)
-
-    cov_copies = []
-    for d in range(1, n_epoch):
-        cov_copies.append(to_epoch(
-            cov_held.at[me], cov_held.at[me], cov_send.at[d - 1], cov_recv.at[me],
-            (me + d) % n_epoch,
-        ))
-    def image_to(d):
-        return to_epoch(
-            images, held.at[me], img_send.at[d], img_recv.at[me], partner(d) * 2 + core
-        )
-
-    to_sibling = to_epoch(images, held.at[me], img_send.at[0], img_recv.at[me], sibling)
-    first, second = 1 + core, 2 - core
-    start_now = [image_to(first)] if relay else [image_to(d) for d in range(1, n_chip)]
-    row_copies = []
-    for d in range(1, n_tile):
-        row_copies.append(to_tile(
-            cov_rows.at[z], cov_rows.at[z], row_send.at[d - 1], row_recv.at[z],
-            (z + d) % n_tile,
-        ))
-    for copy in start_now + [to_sibling] + cov_copies + row_copies:
-        copy.start()
 
     def image_block(block):
         return to_epoch(

time: 62.3 us -> 62.3 us (level)
  no operation moved by 1% of the time
where the time goes in v7:
time: 62.3 us; the launch traced here: 62.2 us
  Pallas kernels  59.3 us (95%)
  local copies, waits for them, and re-layouts  2.26 us (4%)
  between operations  0.65 us (1%)
    pallas_call x1, Pallas kernels, body(): pl.pallas_call(functools.partial(kernel, n_epoch, n_tile), out_shape=(out...  59.3 us
    unnamed x4, local copies, waits for them, and re-layouts  2.26 us

profile of v7, /device:TPU:8, one launch (start us, length us, event | category | flops | bytes accessed | tf_op | source)
XLA Modules:
  0.0 62.2 jit_solution(17311179039163044425)
XLA Ops:
  0.6 59.3 %shard_map.41 = (f32[128,256]{1,0:T(8,128)}, f32[128,256]{1,0:T(8,128)}) custom-call(bf16[128,2048]{1,0:T(8,128)(2,1)} %images.1, s32[16,128]{1,0:T(8,128)} %bitcast.1), custom_call_target="tpu_custom_call" | custom-call | tf_op jit(solution)/shard_map/pallas_call | solution.py:403
  59.9 0.0 copy-start
  59.9 1.6 %copy.6 = f32[128,256]{1,0:T(8,128)} copy(f32[128,256]{1,0:T(8,128)} %get-tuple-element.4) | data formatting | bytes 262144
  61.5 0.0 copy-done
  61.5 0.7 %copy.7 = f32[128,256]{1,0:T(8,128)} copy(f32[128,256]{1,0:T(8,128)S(1)} %copy-done) | data formatting | bytes 262144
Async XLA Ops:
  59.9 1.6 %copy-start = (f32[128,256]{1,0:T(8,128)S(1)}, f32[128,256]{1,0:T(8,128)}, u32[]{:S(2)}) copy-start(f32[128,256]{1,0:T(8,128)} %get-tuple-element.5) | copy-start | bytes 393220

commit v8 on v6

--- a/solution.py
+++ b/solution.py
@@ -307,7 +307,7 @@
 
         lax.fori_loop(0, n_tile, overlap, 0)
 
-    lag = 2
+    lag = 1
 
     def step(n, carry):
         @pl.when(n < n_epoch)

time: 62.3 us -> 66.2 us (1.063)
  the two profiles are of different devices: /device:TPU:8 before, /device:TPU:13 now
where the time goes in v8:
time: 66.2 us; the launch traced here: 66 us
  Pallas kernels  63.1 us (95%)
  local copies, waits for them, and re-layouts  2.26 us (3%)
    pallas_call x1, Pallas kernels, body(): pl.pallas_call(functools.partial(kernel, n_epoch, n_tile), out_shape=(out...  63.1 us
    unnamed x4, local copies, waits for them, and re-layouts  2.26 us

profile of v8, /device:TPU:13, one launch (start us, length us, event | category | flops | bytes accessed | tf_op | source)
XLA Modules:
  0.0 66.0 jit_solution(1960014252809815222)
XLA Ops:
  0.6 63.1 %shard_map.41 = (f32[128,256]{1,0:T(8,128)}, f32[128,256]{1,0:T(8,128)}) custom-call(bf16[128,2048]{1,0:T(8,128)(2,1)} %images.1, s32[16,128]{1,0:T(8,128)} %bitcast.1), custom_call_target="tpu_custom_call" | custom-call | tf_op jit(solution)/shard_map/pallas_call | solution.py:398
  63.8 0.0 copy-start
  63.8 1.6 %copy.6 = f32[128,256]{1,0:T(8,128)} copy(f32[128,256]{1,0:T(8,128)} %get-tuple-element.4) | data formatting | bytes 262144
  65.4 0.0 copy-done
  65.4 0.7 copy.7
Async XLA Ops:
  63.8 1.6 %copy-start = (f32[128,256]{1,0:T(8,128)S(1)}, f32[128,256]{1,0:T(8,128)}, u32[]{:S(2)}) copy-start(f32[128,256]{1,0:T(8,128)} %get-tuple-element.5) | copy-start | bytes 393220
